TPU v7x, 128 devices: a whole 4x4x4 slice. The times are simulated.
128 devices in a mesh: row: 8 (over x, core), col: 16 (over z, y).
Axes of the slice: x: 4, y: 4, z: 4, core: 2. Of those that a mesh axis runs over, the one named last changes fastest.
Arguments:
- markov: bfloat16 [2, 512, 128, 128], P(None, 'col'), may hold values from -6 to 6
- omega: bfloat16 [65536, 64], P('col'), may hold values from -0.0234375 to 0.0234375
Outputs:
- denoised: float32 [2, 512, 128, 128], P(None, 'col')
All inputs are finite; a program needn't handle non-finite values.
Results may differ from a plain program's by a relative error of at most 0.0007.
Values may be sent and summed in bfloat16 or wider, within the bound.
A program may use at most 64 MiB of HBM per device.

v0:
```python
import jax
import jax.numpy as jnp
from jax import lax
from jax.sharding import PartitionSpec as P

NS_STEPS = 8


norm_floor = 1e-06
highest = lax.Precision.HIGHEST


def shifted(block, axis, distance):
    devices = range(lax.axis_size(axis))
    route = [((i - distance) % len(devices), i) for i in devices]
    return lax.ppermute(block, axis, route)


def column_gram(matrix):
    return lax.dot_general(
        matrix,
        matrix,
        (((0,), (0,)), ((), ())),
        precision=highest,
        preferred_element_type=jnp.float32,
    )


def square_mul(left, right):
    return jnp.dot(left, right, precision=highest, preferred_element_type=jnp.float32)


def total_gram(partial_value):
    return lax.psum(partial_value, "row")


def orthonormal(sketch):
    gram = total_gram(column_gram(sketch))
    scale = 1.0 / jnp.sqrt(jnp.trace(gram) + norm_floor)
    current = sketch * scale
    inner = gram * (scale * scale)
    for sweep in range(NS_STEPS):
        if sweep > 0:
            inner = total_gram(column_gram(current))
        current = 1.5 * current - 0.5 * square_mul(current, inner)
    return current


def pick_half(pair, half_id):
    return jnp.where(half_id == 0, pair[0], pair[1])


def lag_sums(basis_blocks, column_rows, column_count):
    row_count, out_rows, rank_extent = basis_blocks.shape
    input_columns = column_rows.shape[1] // column_count
    start_total = jnp.zeros((out_rows, row_count + column_count, input_columns), jnp.float32)

    def add_row(row_position, running):
        orthonormal_row_vector = lax.dynamic_index_in_dim(
            basis_blocks, row_position, 0, keepdims=False
        )
        product = jnp.dot(orthonormal_row_vector, column_rows, preferred_element_type=jnp.float32)
        product = product.reshape(out_rows, column_count, input_columns)
        current_sum = lax.dynamic_slice_in_dim(running, row_position, column_count, 1)
        return lax.dynamic_update_slice_in_dim(running, current_sum + product, row_position, 1)

    return lax.fori_loop(0, row_count, add_row, start_total)


def local(markov, omega):
    n_rows = lax.axis_size("row")
    n_cols = lax.axis_size("col")
    row_position = lax.axis_index("row")
    col_id = lax.axis_index("col")
    halves, blocks, out_rows, input_columns = markov.shape
    rank_extent = omega.shape[1]
    bit_count = (n_rows - 1).bit_length()
    held = markov
    for bit_pos in range(bit_count):
        moved = shifted(held, "col", -(1 << bit_pos))
        held = jnp.where(row_position // (1 << bit_pos) % 2 == 1, moved, held)
    following = shifted(held, "col", -1)
    first_block = row_position + col_id
    window = jnp.concatenate(
        [pick_half(held, first_block // n_cols), pick_half(following, (first_block + 1) // n_cols)],
        axis=0,
    )
    omega_blocks = omega.reshape(blocks, input_columns, rank_extent)

    def slab_at(column_id):
        return lax.dynamic_slice_in_dim(window, column_id, blocks, 0).reshape(
            blocks * out_rows, input_columns
        )

    def range_step(column_id, running):
        weights = lax.dynamic_index_in_dim(omega_blocks, column_id, 0, keepdims=False)
        return running + jnp.dot(slab_at(column_id), weights, preferred_element_type=jnp.float32)

    partial_value = lax.fori_loop(
        0, blocks, range_step, jnp.zeros((blocks * out_rows, rank_extent), jnp.float32)
    )
    sketch = lax.psum(partial_value, "col")
    basis = orthonormal(sketch).astype(jnp.bfloat16)

    def projection_update(column_id, running):
        term = lax.dot_general(
            basis, slab_at(column_id), (((0,), (0,)), ((), ())), preferred_element_type=jnp.float32
        )
        return lax.dynamic_update_slice_in_dim(running, term, column_id * input_columns, 1)

    projected_matrix = lax.fori_loop(
        0, blocks, projection_update, jnp.zeros((rank_extent, blocks * input_columns), jnp.float32)
    )
    projected_matrix = lax.psum(projected_matrix, "row").astype(jnp.bfloat16)
    basis_blocks = basis.reshape(blocks, out_rows, rank_extent)
    local_sums = lag_sums(basis_blocks, projected_matrix, blocks).transpose(1, 0, 2)
    for bit_pos in range(bit_count):
        moved = shifted(local_sums.astype(jnp.bfloat16), "col", 1 << bit_pos).astype(
            local_sums.dtype
        )
        local_sums = jnp.where(row_position // (1 << bit_pos) % 2 == 1, moved, local_sums)
    carried = shifted(local_sums[blocks:].astype(jnp.bfloat16), "col", 1).astype(jnp.float32)
    own_half = (col_id < row_position).astype(jnp.int32)
    prev_col = (col_id + n_cols - 1) % n_cols
    carry_half = (prev_col + n_cols * (prev_col < row_position).astype(jnp.int32) + 1) // n_cols
    owned = jnp.stack(
        [
            jnp.where(own_half == half_id, local_sums[:blocks], 0.0)
            + jnp.where(carry_half == half_id, carried, 0.0)
            for half_id in range(2)
        ]
    )
    totals = lax.psum(owned, "row")
    total_rows = blocks * n_rows
    total_cols = blocks * n_cols
    lag_ids = (
        jnp.arange(2, dtype=jnp.int32)[:, None] * total_cols
        + col_id * blocks
        + jnp.arange(blocks, dtype=jnp.int32)[None, :]
    )
    counts = jnp.maximum(
        jnp.minimum(lag_ids, total_rows - 1) - jnp.maximum(0, lag_ids - total_cols + 1) + 1, 0
    )
    counts_f = counts.astype(jnp.float32)[:, :, None, None]
    measured = markov.astype(jnp.float32)
    averaged = totals / jnp.maximum(counts_f, 1.0)
    return jnp.where(counts_f > 0, 0.5 * measured + 0.5 * averaged, measured)


def solution(mesh):
    in_specs = (P(None, "col", None, None), P("col", None))
    out_specs = P(None, "col", None, None)
    return jax.shard_map(local, mesh=mesh, in_specs=in_specs, out_specs=out_specs, check_vma=False)
```

profile of v0, /device:TPU:33, one launch (start us, length us, event | category | flops | bytes accessed | tf_op | source)
XLA Modules:
  0.0 1081.5 jit_solution(9234383871132882267)
XLA Ops:
  8.8 44.6 %collective-permute-done = bf16[2,32,128,128]{3,2,1,0:T(8,128)(2,1)} collective-permute-done((bf16[2,32,128,128]{3,2,1,0:T(8,128)(2,1)}, bf16[2,32,128,128]{3,2,1,0:T(8,128)(2,1)}, u32[]{:S(2)}, u32[]{:S(2)}) %collective-permute-start) | collective-permute-done | bytes 2097184 | tf_op jit(solution)/shard_map/ppermute | solution.py:16
  57.7 44.8 %collective-permute-done.1 = bf16[2,32,128,128]{3,2,1,0:T(8,128)(2,1)} collective-permute-done((bf16[2,32,128,128]{3,2,1,0:T(8,128)(2,1)S(1)}, bf16[2,32,128,128]{3,2,1,0:T(8,128)(2,1)}, u32[]{:S(2)}, u32[]{:S(2)}) %collective-permute-start.1) | collective-permute-done | bytes 2097184 | tf_op jit(solution)/shard_map/ppermute | solution.py:16
  104.3 3.8 collective-permute-start.2
  108.2 42.5 %collective-permute-done.2 = bf16[2,32,128,128]{3,2,1,0:T(8,128)(2,1)} collective-permute-done((bf16[2,32,128,128]{3,2,1,0:T(8,128)(2,1)S(1)}, bf16[2,32,128,128]{3,2,1,0:T(8,128)(2,1)}, u32[]{:S(2)}, u32[]{:S(2)}) %collective-permute-start.2) | collective-permute-done | bytes 2097184 | tf_op jit(solution)/shard_map/ppermute | solution.py:16
  152.1 7.6 collective-permute-start.3
  162.8 38.9 %collective-permute-done.3 = bf16[2,32,128,128]{3,2,1,0:T(8,128)(2,1)S(1)} collective-permute-done((bf16[2,32,128,128]{3,2,1,0:T(8,128)(2,1)}, bf16[2,32,128,128]{3,2,1,0:T(8,128)(2,1)S(1)}, u32[]{:S(2)}, u32[]{:S(2)}) %collective-permute-start.3) | collective-permute-done | bytes 2097184 | tf_op jit(solution)/shard_map/ppermute | solution.py:16
  201.9 92.8 %while.42 = (s32[]{:T(128)}, f32[4096,64]{0,1:T(8,128)}, bf16[64,128,128]{2,1,0:T(8,128)(2,1)S(1)}, bf16[32,128,64]{2,1,0:T(8,128)(2,1)}, s32[]{:T(128)}, /*index=5*/s32[]{:T(128)}) while((s32[]{:T(128)}, f32[4096,64]{0,1:T(8,128)}, bf16[64,128,128]{2,1,0:T(8,128)(2,1)S(1)}, bf16[32,128,64]{2,1,0:T(8,128)(2,1)}, s32[]{:T(128)}, ...), condition=%wide.region_1.2_spmd.clone, body=%wide.region_0.1_spmd.clone.sunk | while | flops 67633152 | bytes 5276243 | solution.py:99
  294.8 94.8 %all-reduce.4.cloned.1.call-done = f32[4096,64]{0,1:T(8,128)} async-done(((f32[4096,64]{0,1:T(8,128)}), f32[4096,64]{0,1:T(8,128)}) %all-reduce.4.cloned.1.call-update) | async-done | bytes 1048592 | tf_op jit(solution)/shard_map/psum | solution.py:102
  392.1 22.7 %psum.78 = f32[64,64]{1,0:T(8,128)S(1)} all-reduce(f32[64,64]{1,0:T(8,128)S(1)} %fusion.31), channel_id=1, replica_groups=mesh['row'=8,'col'=16] {'row'}, use_global_device_ids=true, to_apply=%region_3.4 | all-reduce | flops 4096 | bytes 32768 | tf_op jit(solution)/shard_map/psum | solution.py:34
  419.8 23.6 %psum.79 = f32[64,64]{1,0:T(8,128)S(1)} all-reduce(f32[64,64]{1,0:T(8,128)S(1)} %fusion.32), channel_id=1, replica_groups=mesh['row'=8,'col'=16] {'row'}, use_global_device_ids=true, to_apply=%region_5.6 | all-reduce | flops 4096 | bytes 32768 | tf_op jit(solution)/shard_map/psum | solution.py:34
  446.5 23.6 %psum.80 = f32[64,64]{1,0:T(8,128)S(1)} all-reduce(f32[64,64]{1,0:T(8,128)S(1)} %fusion.33), channel_id=1, replica_groups=mesh['row'=8,'col'=16] {'row'}, use_global_device_ids=true, to_apply=%region_6.7 | all-reduce | flops 4096 | bytes 32768 | tf_op jit(solution)/shard_map/psum | solution.py:34
  473.7 23.8 %psum.81 = f32[64,64]{1,0:T(8,128)S(1)} all-reduce(f32[64,64]{1,0:T(8,128)S(1)} %fusion.34), channel_id=1, replica_groups=mesh['row'=8,'col'=16] {'row'}, use_global_device_ids=true, to_apply=%region_7.8 | all-reduce | flops 4096 | bytes 32768 | tf_op jit(solution)/shard_map/psum | solution.py:34
  500.5 23.6 %psum.82 = f32[64,64]{1,0:T(8,128)S(1)} all-reduce(f32[64,64]{1,0:T(8,128)S(1)} %fusion.35), channel_id=1, replica_groups=mesh['row'=8,'col'=16] {'row'}, use_global_device_ids=true, to_apply=%region_8.9 | all-reduce | flops 4096 | bytes 32768 | tf_op jit(solution)/shard_map/psum | solution.py:34
  527.8 23.6 %psum.83 = f32[64,64]{1,0:T(8,128)S(1)} all-reduce(f32[64,64]{1,0:T(8,128)S(1)} %fusion.36), channel_id=1, replica_groups=mesh['row'=8,'col'=16] {'row'}, use_global_device_ids=true, to_apply=%region_9.10 | all-reduce | flops 4096 | bytes 32768 | tf_op jit(solution)/shard_map/psum | solution.py:34
  554.4 23.6 %psum.84 = f32[64,64]{1,0:T(8,128)S(1)} all-reduce(f32[64,64]{1,0:T(8,128)S(1)} %fusion.37), channel_id=1, replica_groups=mesh['row'=8,'col'=16] {'row'}, use_global_device_ids=true, to_apply=%region_10.11 | all-reduce | flops 4096 | bytes 32768 | tf_op jit(solution)/shard_map/psum | solution.py:34
  581.6 23.6 %psum.85 = f32[64,64]{1,0:T(8,128)S(1)} all-reduce(f32[64,64]{1,0:T(8,128)S(1)} %fusion.38), channel_id=1, replica_groups=mesh['row'=8,'col'=16] {'row'}, use_global_device_ids=true, to_apply=%region_11.12 | all-reduce | flops 4096 | bytes 32768 | tf_op jit(solution)/shard_map/psum | solution.py:34
  611.6 39.2 %while.40 = (s32[]{:T(128)}, f32[64,4096]{1,0:T(8,128)}, bf16[64,128,128]{2,1,0:T(8,128)(2,1)S(1)}, bf16[4096,64]{1,0:T(8,128)(2,1)S(1)}, s32[]{:T(128)}, /*index=5*/s32[]{:T(128)}, s32[]{:T(128)}, s32[]{:T(128)}) while((s32[]{:T(128)}, f32[64,4096]{1,0:T(8,128)}, bf16[64,128,128]{2,1,0:T(8,128)(2,1)S(1)}, bf16[4096,64]{1,0:T(8,128)(2,1)S(1)}, ...), condition=%wide.region_13.14_spmd, body=%wide.region_12.13_spmd.sunk | while | flops 67108872 | bytes 3702923 | solution.py:111
  650.9 53.4 %all-reduce.7 = bf16[64,4096]{1,0:T(8,128)(2,1)S(1)} all-reduce(f32[64,4096]{1,0:T(8,128)} %get-tuple-element.243), channel_id=1, replica_groups=mesh['row'=8,'col'=16] {'row'}, use_global_device_ids=true, to_apply=%region_14.15 | all-reduce | flops 262144 | bytes 1572864 | tf_op jit(solution)/shard_map/psum | solution.py:114
  706.8 108.3 %while.41 = (s32[]{:T(128)}, f32[128,64,128]{2,0,1:T(8,128)}, bf16[32,128,64]{1,2,0:T(8,128)(2,1)}, bf16[64,4096]{1,0:T(8,128)(2,1)S(1)}, s32[]{:T(128)}) while((s32[]{:T(128)}, f32[128,64,128]{2,0,1:T(8,128)}, bf16[32,128,64]{1,2,0:T(8,128)(2,1)}, bf16[64,4096]{1,0:T(8,128)(2,1)S(1)}, s32[]{:T(128)}) %tuple.87), condition=%wide.region_16.17_spmd, body=%wide.region_15.16_spmd.sunk | while | flops 67633152 | bytes 4736061 | solution.py:67
  710.2 3.4 add_dynamic-update-slice_fusion.2
  713.5 3.4 add_dynamic-update-slice_fusion.2
  716.9 3.4 add_dynamic-update-slice_fusion.2
  720.3 3.4 add_dynamic-update-slice_fusion.2
  723.7 3.4 add_dynamic-update-slice_fusion.2
  730.5 3.4 add_dynamic-update-slice_fusion.2
  733.9 3.4 add_dynamic-update-slice_fusion.2
  737.2 3.4 add_dynamic-update-slice_fusion.2
  740.6 3.4 add_dynamic-update-slice_fusion.2
  744.0 3.4 add_dynamic-update-slice_fusion.2
  750.8 3.4 add_dynamic-update-slice_fusion.2
  754.2 3.4 add_dynamic-update-slice_fusion.2
  757.6 3.4 add_dynamic-update-slice_fusion.2
  760.9 3.4 add_dynamic-update-slice_fusion.2
  764.3 3.4 add_dynamic-update-slice_fusion.2
  767.7 3.4 add_dynamic-update-slice_fusion.2
  774.5 3.4 add_dynamic-update-slice_fusion.2
  777.9 3.4 add_dynamic-update-slice_fusion.2
  781.3 3.4 add_dynamic-update-slice_fusion.2
  784.6 3.4 add_dynamic-update-slice_fusion.2
  788.0 3.4 add_dynamic-update-slice_fusion.2
  794.8 3.4 add_dynamic-update-slice_fusion.2
  798.2 3.4 add_dynamic-update-slice_fusion.2
  818.2 47.7 %collective-permute-done.4 = bf16[64,128,128]{2,1,0:T(8,128)(2,1)S(1)} collective-permute-done((bf16[64,128,128]{2,1,0:T(8,128)(2,1)S(1)}, bf16[64,128,128]{2,1,0:T(8,128)(2,1)S(1)}, u32[]{:S(2)}, u32[]{:S(2)}) %collective-permute-start.4) | collective-permute-done | bytes 2097184 | tf_op jit(solution)/shard_map/ppermute | solution.py:16
  866.8 47.4 %collective-permute-done.5 = bf16[64,128,128]{2,1,0:T(8,128)(2,1)S(1)} collective-permute-done((bf16[64,128,128]{2,1,0:T(8,128)(2,1)S(1)}, bf16[64,128,128]{2,1,0:T(8,128)(2,1)S(1)}, u32[]{:S(2)}, u32[]{:S(2)}) %collective-permute-start.5) | collective-permute-done | bytes 2097184 | tf_op jit(solution)/shard_map/ppermute | solution.py:16
  916.2 45.8 %collective-permute-done.6 = bf16[64,128,128]{2,1,0:T(8,128)(2,1)S(1)} collective-permute-done((bf16[64,128,128]{2,1,0:T(8,128)(2,1)S(1)}, bf16[64,128,128]{2,1,0:T(8,128)(2,1)S(1)}, u32[]{:S(2)}, u32[]{:S(2)}) %collective-permute-start.6) | collective-permute-done | bytes 2097184 | tf_op jit(solution)/shard_map/ppermute | solution.py:16
  965.8 23.0 %collective-permute-done.7 = bf16[32,128,128]{2,1,0:T(8,128)(2,1)S(1)} collective-permute-done((bf16[32,128,128]{2,1,0:T(8,128)(2,1)S(1)}, bf16[32,128,128]{2,1,0:T(8,128)(2,1)S(1)}, u32[]{:S(2)}, u32[]{:S(2)}) %collective-permute-start.7) | collective-permute-done | bytes 1048608 | tf_op jit(solution)/shard_map/ppermute | solution.py:16
  993.5 76.1 %all-reduce.6.cloned.1.call-done = f32[2,32,128,128]{3,2,1,0:T(8,128)} async-done(((f32[2,32,128,128]{3,2,1,0:T(8,128)}), f32[2,32,128,128]{3,2,1,0:T(8,128)}) %all-reduce.6.cloned.1.call-update) | async-done | bytes 4194320 | tf_op jit(solution)/shard_map/psum | solution.py:133
  1069.7 5.0 convert_select_fusion
  (202 shorter events, 225.0 us)
Async XLA Ops:
  6.5 383.0 %all-reduce.4.cloned.1.call-start = ((), (), s32[]{:S(2)}) async-start(), calls=%async_computation | async-start | bytes 2097152 | tf_op jit(solution)/shard_map/psum | solution.py:102
  6.5 46.9 %collective-permute-start = (bf16[2,32,128,128]{3,2,1,0:T(8,128)(2,1)}, bf16[2,32,128,128]{3,2,1,0:T(8,128)(2,1)}, u32[]{:S(2)}, u32[]{:S(2)}) collective-permute-start(bf16[2,32,128,128]{3,2,1,0:T(8,128)(2,1)} %param.8), channel_id=1, source_target_pairs={{1,0},{2,1},{3,2},{4,3},{5,4},{6,5},{7,6},{8,7},{9,8},{10,9},{11,1... | collective-permute-start | bytes 6291464 | tf_op jit(solution)/shard_map/ppermute | solution.py:16
  55.2 2.5 copy-start.5
  55.3 47.3 %collective-permute-start.1 = (bf16[2,32,128,128]{3,2,1,0:T(8,128)(2,1)S(1)}, bf16[2,32,128,128]{3,2,1,0:T(8,128)(2,1)}, u32[]{:S(2)}, u32[]{:S(2)}) collective-permute-start(bf16[2,32,128,128]{3,2,1,0:T(8,128)(2,1)S(1)} %broadcast_select_fusion), channel_id=1, source_target_pairs={{2,0},{3,1},{4,2},{5,3},{6,4},{7,5},{8,6},{9,7},{10,8},{11,9},{12,... | collective-permute-start | bytes 6291464 | tf_op jit(solution)/shard_map/ppermute | solution.py:16
  104.3 46.3 %collective-permute-start.2 = (bf16[2,32,128,128]{3,2,1,0:T(8,128)(2,1)S(1)}, bf16[2,32,128,128]{3,2,1,0:T(8,128)(2,1)}, u32[]{:S(2)}, u32[]{:S(2)}) collective-permute-start(bf16[2,32,128,128]{3,2,1,0:T(8,128)(2,1)S(1)} %broadcast_select_fusion.1), channel_id=1, source_target_pairs={{4,0},{5,1},{6,2},{7,3},{8,4},{9,5},{10,6},{11,7},{12,8},{13,9},{1... | collective-permute-start | bytes 6291464 | tf_op jit(solution)/shard_map/ppermute | solution.py:16
  108.2 51.6 %copy-start.7 = (bf16[4096,64]{0,1:T(8,128)(2,1)S(1)}, bf16[4096,64]{0,1:T(8,128)(2,1)}, u32[]{:S(2)}) copy-start(bf16[4096,64]{0,1:T(8,128)(2,1)} %param.9) | copy-start | bytes 1572868
  152.1 49.5 %collective-permute-start.3 = (bf16[2,32,128,128]{3,2,1,0:T(8,128)(2,1)}, bf16[2,32,128,128]{3,2,1,0:T(8,128)(2,1)S(1)}, u32[]{:S(2)}, u32[]{:S(2)}) collective-permute-start(bf16[2,32,128,128]{3,2,1,0:T(8,128)(2,1)} %broadcast_select_fusion.2), channel_id=1, source_target_pairs={{1,0},{2,1},{3,2},{4,3},{5,4},{6,5},{7,6},{8,7},{9,8},{10,9},{11,1... | collective-permute-start | bytes 6291464 | tf_op jit(solution)/shard_map/ppermute | solution.py:16
  294.7 774.9 %all-reduce.6.cloned.1.call-start = ((), (), s32[]{:S(2)}) async-start(), calls=%async_computation.1 | async-start | bytes 8388608 | tf_op jit(solution)/shard_map/psum | solution.py:133
  444.6 1.0 copy-start.1
  498.6 1.0 copy-start.2
  552.5 1.0 copy-start.3
  815.1 50.8 %copy-start = (f32[128,64,128]{2,0,1:T(8,128)S(1)}, f32[128,64,128]{2,0,1:T(8,128)}, u32[]{:S(2)}) copy-start(f32[128,64,128]{2,0,1:T(8,128)} %get-tuple-element.244) | copy-start | bytes 12582916
  817.8 48.1 %collective-permute-start.4 = (bf16[64,128,128]{2,1,0:T(8,128)(2,1)S(1)}, bf16[64,128,128]{2,1,0:T(8,128)(2,1)S(1)}, u32[]{:S(2)}, u32[]{:S(2)}) collective-permute-start(bf16[64,128,128]{2,1,0:T(8,128)(2,1)S(1)} %bitcast_convert_fusion), channel_id=1, source_target_pairs={{15,0},{0,1},{1,2},{2,3},{3,4},{4,5},{5,6},{6,7},{7,8},{8,9},{9,10... | collective-permute-start | bytes 6291464 | tf_op jit(solution)/shard_map/ppermute | solution.py:16
  866.8 47.5 %collective-permute-start.5 = (bf16[64,128,128]{2,1,0:T(8,128)(2,1)S(1)}, bf16[64,128,128]{2,1,0:T(8,128)(2,1)S(1)}, u32[]{:S(2)}, u32[]{:S(2)}) collective-permute-start(bf16[64,128,128]{2,1,0:T(8,128)(2,1)S(1)} %fusion.24), channel_id=1, source_target_pairs={{14,0},{15,1},{0,2},{1,3},{2,4},{3,5},{4,6},{5,7},{6,8},{7,9},{8,1... | collective-permute-start | bytes 6291464 | tf_op jit(solution)/shard_map/ppermute | solution.py:16
  915.5 46.5 %collective-permute-start.6 = (bf16[64,128,128]{2,1,0:T(8,128)(2,1)S(1)}, bf16[64,128,128]{2,1,0:T(8,128)(2,1)S(1)}, u32[]{:S(2)}, u32[]{:S(2)}) collective-permute-start(bf16[64,128,128]{2,1,0:T(8,128)(2,1)S(1)} %fusion.19), channel_id=1, source_target_pairs={{12,0},{13,1},{14,2},{15,3},{0,4},{1,5},{2,6},{3,7},{4,8},{5,9},{6... | collective-permute-start | bytes 6291464 | tf_op jit(solution)/shard_map/ppermute | solution.py:16
  963.5 2.0 copy-start.4
  965.7 23.1 %collective-permute-start.7 = (bf16[32,128,128]{2,1,0:T(8,128)(2,1)S(1)}, bf16[32,128,128]{2,1,0:T(8,128)(2,1)S(1)}, u32[]{:S(2)}, u32[]{:S(2)}) collective-permute-start(bf16[32,128,128]{2,1,0:T(8,128)(2,1)S(1)} %slice.43), channel_id=1, source_target_pairs={{15,0},{0,1},{1,2},{2,3},{3,4},{4,5},{5,6},{6,7},{7,8},{8,9},{9,10... | collective-permute-start | bytes 3145736 | tf_op jit(solution)/shard_map/ppermute | solution.py:16
  993.3 76.3 %copy-start.6 = (bf16[2,32,128,128]{3,2,1,0:T(8,128)(2,1)S(1)}, bf16[2,32,128,128]{3,2,1,0:T(8,128)(2,1)}, u32[]{:S(2)}) copy-start(bf16[2,32,128,128]{3,2,1,0:T(8,128)(2,1)} %param.8) | copy-start | bytes 6291460
Sparse Core Ops, SparseCore 0:
  294.9 94.6 all-reduce.3
  993.5 76.1 all-reduce.5
where the time goes:
time: 1090 us; the launch traced here: 1080 us
  waiting for transfers between devices  506 us (46%)
  matrix products  258 us (24%)
  blocking collectives  241 us (22%)
  other arithmetic  23.7 us (2%)
  local copies, waits for them, and re-layouts  19.9 us (2%)
  starting transfers between devices  17.4 us (2%)
  between operations  14.4 us (1%)
    ppermute x8, waiting for transfers between devices, shifted(): return lax.ppermute(block, axis, route)  335 us
    psum x8, blocking collectives, total_gram(): return lax.psum(partial_value, 'row')  188 us
    dot_general x32, matrix products, add_row(): jnp.dot(orthonormal_row_vector, column_rows, preferred_element_type=jnp.f...  108 us
    psum x1, waiting for transfers between devices, local(): sketch = lax.psum(partial_value, 'col')  94.8 us
    dot_general x32, matrix products, range_step(): jnp.dot(slab_at(column_id), weights, preferred_element_type=jnp.float32)  89.1 us
    psum x1, waiting for transfers between devices, local(): totals = lax.psum(owned, 'row')  76.1 us
    psum x1, blocking collectives, local(): projected_matrix = lax.psum(projected_matrix, 'row').astype(jnp.bfloat16)  53.4 us
    dot_general x32, matrix products, projection_update(): lax.dot_general(basis, slab_at(column_id), (((0,), (0,)), ((), ())), pref...  35.7 us
  transfers between devices with their start and end apart: 10, of which 10 were waited for; matrix products, arithmetic and copies ran while one was open for 0% of the time, Pallas kernels for 0%

commit v1 on v0

v1 whole, which is shorter than its diff:
```python
import functools

import jax
import jax.numpy as jnp
from jax import lax
from jax.experimental import pallas as pl
from jax.experimental.pallas import tpu as pltpu
from jax.sharding import PartitionSpec as P

NS_STEPS = 8
norm_floor = 1e-06
highest = lax.Precision.HIGHEST
MESH = pl.DeviceIdType.MESH
KH = 32
B = 128
f32, bf16 = jnp.float32, jnp.bfloat16
NT_DIMS = (((1,), (1,)), ((), ()))


def mm(left, right, **kw):
    return jnp.dot(left, right, preferred_element_type=f32, **kw)


def mm_nt(left, right, **kw):
    return lax.dot_general(left, right, NT_DIMS, preferred_element_type=f32, **kw)


def kernel(
    X, C, nb, SDT,
    l_ref, om_ref, out_ref,
    wl, q, omp, acc, s_send, s_recv, s_full, g_own, gx_recv, g_x, gc_recv, p_ref,
    bp, bpt, pacc, pr_send, pr_recv, prb, prx, tot, tx_send, tx_recv, ch, xr,
    l_sem, om_s, om_r, s_s, s_r, sx_s, sx_r, gx_s, gx_r, gc_s, gc_r, b_s, b_r,
    pr_s, pr_r, pa_s, pa_r, tx_s, tx_r, xr_s, xr_r, ag_s, ag_r, fx_s, fx_r,
):
    NT = nb // 2
    PO = nb // C
    PQ = NT // X
    LQ = NT // X
    r = lax.axis_index("row")
    c = lax.axis_index("col")
    x, core = r // 2, r % 2

    def dev(xx, cc, kk=None):
        return (xx * 2 + (core if kk is None else kk), cc)

    def col(dc):
        return lax.rem(c + dc + 4 * C, C)

    def xat(dx):
        return lax.rem(x + dx, X)

    def xcol(dx, delta):
        xx = xat(dx)
        return dev(xx, lax.rem(c + 2 * (xx - x) + delta + 4 * C, C))

    def remote(src, dst, send, recv, device):
        return pltpu.make_async_remote_copy(
            src_ref=src, dst_ref=dst, send_sem=send, recv_sem=recv, device_id=device, device_id_type=MESH
        )

    halves = [jnp.where(c - 2 * x - e < 0, 1, 0).astype(jnp.int32) for e in range(3)]

    loads = []
    for h in range(2):
        for s in range(2):
            loads.append(
                pltpu.make_async_copy(
                    l_ref.at[h],
                    wl.at[h, pl.ds((1 + s) * B, nb * B), pl.ds(s * B, B)],
                    l_sem.at[2 * h + s],
                )
            )
    for cp in loads:
        cp.start()

    barrier = pltpu.get_barrier_semaphore()
    peers = [dev(x, col(dc)) for dc in range(1, C)]
    for dx in range(1, X):
        peers += [xcol(dx, delta) for delta in (-1, 0, 1)] + [dev(xat(dx), c)]
    peers.append(dev(x, c, 1 - core))
    for peer in peers:
        pl.semaphore_signal(barrier, inc=1, device_id=peer, device_id_type=MESH)

    pick = jnp.where(
        lax.broadcasted_iota(jnp.int32, (KH, 2 * KH), 1)
        == lax.broadcasted_iota(jnp.int32, (KH, 2 * KH), 0) + core * KH,
        1.0, 0.0,
    ).astype(bf16)
    for w in range(NT):
        both = mm_nt(pick, om_ref[w * 2 * B : (w + 1) * 2 * B, :]).astype(bf16)
        n = NT - 1 - w
        q[n * KH : (n + 1) * KH, :B] = both[:, B:]
        q[n * KH : (n + 1) * KH, B:] = both[:, :B]

    pl.semaphore_wait(barrier, len(peers))

    pending = []

    om_self = [lax.rem(2 * x + e, C) == 0 for e in range(3)]
    om_copies = []
    for e in range(3):
        cp = remote(q, omp.at[e], om_s.at[e], om_r.at[e], dev(x, col(2 * x + e)))
        om_copies.append(cp)

        @pl.when(jnp.logical_not(om_self[e]))
        def _():
            cp.start()

        @pl.when(om_self[e])
        def _():
            omp[e] = q[...]

    for h in range(2):
        zero = jnp.zeros((B, B), bf16)
        wl[h, 0:B, 0:B] = zero
        wl[h, 0:B, B:] = zero
        wl[h, B : 2 * B, B:] = zero
        wl[h, (nb + 1) * B :, 0:B] = zero
    bp[0 : NT * KH, :] = jnp.zeros((NT * KH, 2 * B), bf16)
    bp[3 * NT * KH :, :] = jnp.zeros((NT * KH, 2 * B), bf16)
    acc[...] = jnp.zeros_like(acc)
    for cp in loads:
        cp.wait()

    HB = NT // 2
    blocks = {
        0: ((0, HB, HB + 1, NT + 1), (HB, HB, 1, NT + 1)),
        1: ((0, NT, 0, NT + 1),),
        2: ((0, HB, 0, NT), (HB, HB, 0, HB)),
    }

    for e in range(3):
        @pl.when(jnp.logical_not(om_self[e]))
        def _():
            om_copies[e].wait_recv()

        for start, size, lo, hi in blocks[e]:
            rows = size * KH

            def step(tau, carry):
                left = omp[e, start * KH : start * KH + rows, :]
                right = wl[halves[e], pl.ds(pl.multiple_of(tau * 2 * B, 2 * B), 2 * B), :]
                at = pl.ds(pl.multiple_of((e * NT + start + tau) * KH, KH), rows)
                acc[at, :] += mm_nt(left, right)
                return carry

            lax.fori_loop(lo, hi, step, 0)

    s_send[...] = acc[NT * KH : 3 * NT * KH, :].astype(SDT)
    srows = PO * KH
    copies = []
    for dc in range(1, C):
        dst = col(dc)
        cp = remote(
            s_send.at[pl.ds(pl.multiple_of(dst * srows, srows), srows)], s_recv.at[dc],
            s_s.at[dc], s_r.at[dc], dev(x, dst),
        )
        cp.start()
        copies.append(cp)
    total = acc[pl.ds(pl.multiple_of((NT + c * PO) * KH, KH), srows), :]
    for dc in range(1, C):
        copies[dc - 1].wait_recv()
        total = total + s_recv[dc].astype(f32)
    pending += copies
    s_full[core] = total
    cp = remote(s_full.at[core], s_full.at[core], sx_s, sx_r, dev(x, c, 1 - core))
    cp.start()
    cp.wait_recv()
    pending.append(cp)

    sk = jnp.concatenate(
        [
            jnp.concatenate([s_full[k, o * KH : (o + 1) * KH, :] for k in range(2)], axis=0)
            for o in range(PO)
        ],
        axis=1,
    )
    gram = mm_nt(sk, sk, precision=highest)
    g_own[...] = jnp.concatenate([gram[:KH], gram[KH:]], axis=1)
    copies = []
    for dx in range(1, X):
        cp = remote(g_own, gx_recv.at[dx], gx_s.at[dx], gx_r.at[dx], dev(xat(dx), c))
        cp.start()
        copies.append(cp)
    packed = g_own[...]
    for dx in range(1, X):
        copies[dx - 1].wait_recv()
        packed = packed + gx_recv[dx]
    pending += copies
    g_x[...] = packed
    copies = []
    for dc in range(1, C):
        cp = remote(g_x, gc_recv.at[dc], gc_s.at[dc], gc_r.at[dc], dev(x, col(dc)))
        cp.start()
        copies.append(cp)
    for dc in range(1, C):
        copies[dc - 1].wait_recv()
        packed = packed + gc_recv[dc]
    pending += copies
    gram = jnp.concatenate([packed[:, : 2 * KH], packed[:, 2 * KH :]], axis=0)

    eye = (
        lax.broadcasted_iota(jnp.int32, (2 * KH, 2 * KH), 0)
        == lax.broadcasted_iota(jnp.int32, (2 * KH, 2 * KH), 1)
    ).astype(f32)
    trace = jnp.sum(gram * eye)
    scale = 1.0 / jnp.sqrt(jnp.full((1, 1), trace, f32) + norm_floor)
    inner = gram * (scale * scale)
    prod = None
    for sweep in range(NS_STEPS):
        a = 1.5 * eye - 0.5 * inner
        prod = a if prod is None else mm(prod, a, precision=highest)
        if sweep < NS_STEPS - 1:
            inner = mm(a, mm(inner, a, precision=highest), precision=highest)
    p_ref[...] = prod * scale

    basis = mm(p_ref[pl.ds(pl.multiple_of(core * KH, KH), KH), :], sk, precision=highest).astype(bf16)
    mine = pl.multiple_of((NT + c * PO) * KH, KH)
    for o in range(PO):
        bp[pl.ds(pl.multiple_of(mine + o * KH, KH), KH), :] = basis[:, o * 2 * B : (o + 1) * 2 * B]
    copies = []
    for dc in range(1, C):
        at = bp.at[pl.ds(mine, srows)]
        cp = remote(at, at, b_s.at[dc], b_r.at[dc], dev(x, col(dc)))
        cp.start()
        copies.append(cp)
    for cp in copies:
        cp.wait_recv()
    pending += copies

    qrows = PQ * KH
    pr_copies = {}
    for e in (0, 2, 1):
        pacc[...] = jnp.zeros_like(pacc)
        for start, size, lo, hi in blocks[e]:
            rows = size * KH

            def step(tau, carry):
                at = pl.ds(pl.multiple_of((e * NT + start + tau) * KH, KH), rows)
                right = wl[halves[e], pl.ds(pl.multiple_of(tau * 2 * B, 2 * B), 2 * B), :]
                pacc[start * KH : start * KH + rows, :] += mm(bp[at, :], right)
                return carry

            lax.fori_loop(lo, hi, step, 0)
        pr_send[e] = pacc[...].astype(bf16)
        for dx in range(X):
            if dx == 0 and e == 1:
                continue
            slot = dx * 3 + e
            cp = remote(
                pr_send.at[e, pl.ds(pl.multiple_of(xat(dx) * qrows, qrows), qrows)], pr_recv.at[slot],
                pr_s.at[slot], pr_r.at[slot], xcol(dx, 1 - e),
            )
            cp.start()
            pr_copies[slot] = cp

    for g in range(NT):
        first = (NT + 2 * g) * KH
        pieces = [
            bp[first + o * KH : first + (o + 1) * KH, s * B : (s + 1) * B] for o in range(2) for s in range(2)
        ]
        bpt[:, g * B : (g + 1) * B] = jnp.concatenate(pieces, axis=0).T

    quarter = pl.ds(pl.multiple_of(x * qrows, qrows), qrows)
    total = pacc[quarter, :]
    for slot, cp in pr_copies.items():
        cp.wait_recv()
        total = total + pr_recv[slot].astype(f32)
    pending += list(pr_copies.values())
    prb[1, quarter, :] = total.astype(bf16)
    copies = []
    for dx in range(X):
        for e in range(3):
            if dx == 0 and e == 1:
                continue
            slot = dx * 3 + e
            cp = remote(
                prb.at[1, quarter], prb.at[e, quarter], pa_s.at[slot], pa_r.at[slot], xcol(dx, e - 1)
            )
            cp.start()
            copies.append(cp)
    for cp in copies:
        cp.wait_recv()
    pending += copies

    def active(h, xx):
        return c - 2 * xx >= 0 if h == 0 else c - 2 * xx - 2 < 0

    tx_copies = []
    for h in range(2):
        cp = remote(tx_send.at[h], tx_recv.at[h], tx_s.at[h], tx_r.at[h], dev(x, c, 1 - core))
        tx_copies.append(cp)

        @pl.when(active(h, x))
        def _():
            for e in range(3):
                @pl.when(halves[e] == h)
                def _():
                    for i in range(NT):
                        n = e * NT + i
                        pair = prb[e, i * KH : (i + 1) * KH, :]
                        prx[n, 0:KH, :] = pair
                        prx[n, KH:, :B] = pair[:, B:]
                        if n > 0:
                            prx[n - 1, KH:, B:] = pair[:, :B]

                @pl.when(halves[e] != h)
                def _():
                    for i in range(NT):
                        n = e * NT + i
                        prx[n, 0:KH, :] = jnp.zeros((KH, 2 * B), bf16)
                        prx[n, KH:, :B] = jnp.zeros((KH, B), bf16)
                        if n > 0:
                            prx[n - 1, KH:, B:] = jnp.zeros((KH, B), bf16)

            def lag_pair(tp):
                right = prx[pl.ds(NT - 1 - tp, 2 * NT)].reshape(4 * NT * KH, 2 * B)
                return mm(bpt[...], right)

            def other(i, carry):
                value = lag_pair((1 - core) * HB + i).astype(bf16)
                tx_send[h, 2 * i] = value[:, B:]
                tx_send[h, 2 * i + 1] = value[:, :B]
                return carry

            lax.fori_loop(0, HB, other, 0)
            cp.start()

            def this(i, carry):
                value = lag_pair(core * HB + i)
                tot[h, 2 * i] = value[:, B:]
                tot[h, 2 * i + 1] = value[:, :B]
                return carry

            lax.fori_loop(0, HB, this, 0)

    nbr, nbc = 2 * nb * X, nb * C

    def lag_of(h, t):
        return h * nbc + c * nb + core * NT + t

    def pairs_of(lag, first, last):
        low = jnp.maximum(first, lag - (nbc - 1))
        return jnp.maximum(jnp.minimum(last, lag) - low + 1, 0).astype(f32)

    def measured(h, t):
        return wl[h, pl.ds(pl.multiple_of((core * NT + t + 1) * B, B), B), 0:B].astype(f32)

    xr_sends = []
    for h in range(2):
        sends = []
        for dx in range(1, X):
            xx = xat(dx)
            sends.append(
                remote(
                    ch.at[h, pl.ds(xx * LQ, LQ)], xr.at[h, dx], xr_s.at[h * X + dx], xr_r.at[h * X + dx],
                    dev(xx, c),
                )
            )
        xr_sends.append(sends)

        @pl.when(active(h, x))
        def _():
            tx_copies[h].wait_recv()

            def combine(t, carry):
                n = pairs_of(lag_of(h, t), 2 * nb * x, 2 * nb * (x + 1) - 1)
                value = tot[h, t] + tx_recv[h, t].astype(f32) - (0.5 * n) * measured(h, t)
                tot[h, t] = value
                ch[h, t] = value.astype(bf16)
                return carry

            lax.fori_loop(0, NT, combine, 0)
            for cp in sends:
                cp.start()

    ag_copies, fx_copies = [], []
    has = [None, c < 2 * X]
    for h in range(2):
        def finish():
            at0 = core * NT + x * LQ

            @pl.when(jnp.logical_not(active(h, x)))
            def _():
                for i in range(LQ):
                    tot[h, x * LQ + i] = jnp.zeros((B, B), f32)

            for dx in range(1, X):
                src = lax.rem(x - dx + X, X)

                @pl.when(active(h, src))
                def _():
                    xr_sends[h][dx - 1].wait_recv()
                    for i in range(LQ):
                        tot[h, x * LQ + i] += xr[h, dx, i].astype(f32)

            for i in range(LQ):
                n = pairs_of(lag_of(h, x * LQ + i), 0, nbr - 1)
                value = tot[h, x * LQ + i] / jnp.maximum(n, 1.0)
                out_ref[h, at0 + i] = value.astype(bf16)

        at = out_ref.at[h, pl.ds(core * NT + x * LQ, LQ)]
        sends = [
            remote(at, at, ag_s.at[h * X + dx], ag_r.at[h * X + dx], dev(xat(dx), c)) for dx in range(1, X)
        ]
        mine_at = out_ref.at[h, pl.ds(core * NT, NT)]
        across = remote(mine_at, mine_at, fx_s.at[h], fx_r.at[h], dev(x, c, 1 - core))
        ag_copies.append(sends)
        fx_copies.append(across)

        def spread():
            finish()
            for cp in sends:
                cp.start()

        if h == 0:
            spread()
        else:
            pl.when(has[1])(spread)

            @pl.when(jnp.logical_not(has[1]))
            def _():
                out_ref[1] = jnp.zeros((nb, B, B), bf16)

    def gather(h):
        for cp in ag_copies[h]:
            cp.wait_recv()
        fx_copies[h].start()

    gather(0)
    pl.when(has[1])(functools.partial(gather, 1))

    def settle(h):
        fx_copies[h].wait_recv()
        for cp in ag_copies[h]:
            cp.wait_send()
        fx_copies[h].wait_send()

    settle(0)
    pl.when(has[1])(functools.partial(settle, 1))
    for h in range(2):
        @pl.when(active(h, x))
        def _():
            tx_copies[h].wait_send()
            for cp in xr_sends[h]:
                cp.wait_send()

    for e in range(3):
        @pl.when(jnp.logical_not(om_self[e]))
        def _():
            om_copies[e].wait_send()

    for cp in pending:
        cp.wait_send()


def local(X, C, SDT, markov, omega):
    halves, nb = markov.shape[:2]
    NT = nb // 2
    PO, PQ, LQ = nb // C, NT // X, NT // X
    vmem, dma = pltpu.VMEM, pltpu.SemaphoreType.DMA
    scratch = [
        vmem((2, (nb + 2) * B, 2 * B), bf16),
        vmem((NT * KH, 2 * B), bf16),
        vmem((3, NT * KH, 2 * B), bf16),
        vmem(((4 * NT + 1) * KH, 2 * B), f32),
        vmem((2 * NT * KH, 2 * B), SDT),
        vmem((C, PO * KH, 2 * B), SDT),
        vmem((2, PO * KH, 2 * B), f32),
        vmem((KH, 4 * KH), f32),
        vmem((X, KH, 4 * KH), f32),
        vmem((KH, 4 * KH), f32),
        vmem((C, KH, 4 * KH), f32),
        vmem((2 * KH, 2 * KH), f32),
        vmem((4 * NT * KH, 2 * B), bf16),
        vmem((B, NT * B), bf16),
        vmem((NT * KH, 2 * B), f32),
        vmem((3, NT * KH, 2 * B), bf16),
        vmem((3 * X, PQ * KH, 2 * B), bf16),
        vmem((3, NT * KH, 2 * B), bf16),
        vmem((3 * NT, 2 * KH, 2 * B), bf16),
        vmem((2, NT, B, B), f32),
        vmem((2, NT, B, B), bf16),
        vmem((2, NT, B, B), bf16),
        vmem((2, NT, B, B), bf16),
        vmem((2, X, LQ, B, B), bf16),
        dma((4,)),
        dma((3,)), dma((3,)), dma((C,)), dma((C,)), dma, dma,
        dma((X,)), dma((X,)), dma((C,)), dma((C,)), dma((C,)), dma((C,)),
        dma((3 * X,)), dma((3 * X,)), dma((3 * X,)), dma((3 * X,)),
        dma((2,)), dma((2,)), dma((2 * X,)), dma((2 * X,)), dma((2 * X,)), dma((2 * X,)),
        dma((2,)), dma((2,)),
    ]
    excess = pl.pallas_call(
        functools.partial(kernel, X, C, nb, SDT),
        out_shape=jax.ShapeDtypeStruct((halves, nb, B, B), bf16),
        in_specs=[pl.BlockSpec(memory_space=pl.ANY), pl.BlockSpec(memory_space=pltpu.VMEM)],
        out_specs=pl.BlockSpec(memory_space=pltpu.VMEM),
        scratch_shapes=scratch,
        compiler_params=pltpu.CompilerParams(
            collective_id=0, has_side_effects=True, vmem_limit_bytes=48 * 2**20
        ),
        name="cadzow",
    )(markov.reshape(halves, nb * B, B), omega)
    lags = (
        jnp.arange(2, dtype=jnp.int32)[:, None] * (nb * C)
        + lax.axis_index("col") * nb
        + jnp.arange(nb, dtype=jnp.int32)[None, :]
    )
    counts = jnp.minimum(lags, 2 * nb * X - 1) - jnp.maximum(0, lags - nb * C + 1) + 1
    measured = markov.astype(f32)
    merged = 0.75 * measured + 0.5 * excess.astype(f32)
    return jnp.where((counts > 0)[:, :, None, None], merged, measured)


def solution(mesh):
    X, C = mesh.shape["row"] // 2, mesh.shape["col"]
    in_specs = (P(None, "col", None, None), P("col", None))
    return jax.shard_map(
        functools.partial(local, X, C, bf16),
        mesh=mesh,
        in_specs=in_specs,
        out_specs=P(None, "col", None, None),
        check_vma=False,
    )
```

time: 1090 us -> 149 us (0.14)
  waiting for transfers between devices: 506 us -> 0 us
  matrix products: 258 us -> 0 us
  blocking collectives: 241 us -> 0 us
  Pallas kernels: 0 us -> 142 us
  other arithmetic: 23.7 us -> 3.24 us
  starting transfers between devices: 17.4 us -> 0 us
  local copies, waits for them, and re-layouts: 19.9 us -> 3.1 us
  between operations: 14.4 us -> 0.03 us
    ppermute x8 -> x0, waiting for transfers between devices: 335 us -> none  [shifted(): return lax.ppermute(block, axis, route)]
    dot_general x112 -> x0, matrix products: 258 us -> none  [the longest x32 108 us: add_row(): jnp.dot(orthonormal_row_vector, column_rows, preferred_element_type=jnp.f...]
    psum x9 -> x0, blocking collectives: 241 us -> none  [the longest x8 188 us: total_gram(): return lax.psum(partial_value, 'row')]
    psum x2 -> x0, waiting for transfers between devices: 171 us -> none  [the longest x1 94.8 us: local(): sketch = lax.psum(partial_value, 'col')]
    pallas_call x0 -> x1, Pallas kernels: none -> 142 us  [local(): pl.pallas_call(functools.partial(kernel, X, C, nb, SDT), out_shape=jax.Sh...]
    ppermute x8 -> x0, starting transfers between devices: 17.4 us -> none  [shifted(): return lax.ppermute(block, axis, route)]
  transfers between devices with their start and end apart: 10 -> 0, of which waited for: 10 -> 0; matrix products, arithmetic and copies ran while one was open for 0% -> 0% of each run, Pallas kernels for 0% -> 0%
where the time goes in v1:
time: 149 us; the launch traced here: 148 us
  Pallas kernels  142 us (95%)
  other arithmetic  3.24 us (2%)
  local copies, waits for them, and re-layouts  3.1 us (2%)
    pallas_call x1, Pallas kernels, local(): pl.pallas_call(functools.partial(kernel, X, C, nb, SDT), out_shape=jax.Sh...  142 us
    select_n x1, other arithmetic, local(): return jnp.where((counts > 0)[:, :, None, None], merged, measured)  3.15 us
    unnamed x3, local copies, waits for them, and re-layouts  3.1 us

profile of v1, /device:TPU:33, one launch (start us, length us, event | category | flops | bytes accessed | tf_op | source)
XLA Modules:
  0.0 148.3 jit_solution(12772218788527312444)
XLA Ops:
  0.0 0.1 add_compare_fusion
  0.1 1.5 %copy.3.om_ref = bf16[4096,64]{1,0:T(8,128)(2,1)S(1)} copy(bf16[4096,64]{0,1:T(8,128)(2,1)} %param.3) | data formatting | bytes 1048576 | tf_op args[1]
  1.6 0.0 copy-start
  1.6 1.6 %copy-done = bf16[2,32,128,128]{3,2,1,0:T(8,128)(2,1)S(1)} copy-done((bf16[2,32,128,128]{3,2,1,0:T(8,128)(2,1)S(1)}, bf16[2,32,128,128]{3,2,1,0:T(8,128)(2,1)}, u32[]{:S(2)}) %copy-start) | copy-done | bytes 2097176
  3.2 141.9 %cadzow.1 = bf16[2,32,128,128]{3,2,1,0:T(8,128)(2,1)S(1)} custom-call(bf16[2,4096,128]{2,1,0:T(8,128)(2,1)S(1)} %bitcast.1, bf16[4096,64]{1,0:T(8,128)(2,1)S(1)} %copy.3.om_ref), custom_call_target="tpu_custom_call" | custom-call | tf_op jit(solution)/shard_map/cadzow/pallas_call | solution.py:495
  145.1 3.2 %convert_select_fusion = f32[2,32,128,128]{3,2,1,0:T(8,128)} fusion(bf16[2,32,128,128]{3,2,1,0:T(8,128)(2,1)S(1)} %copy-done, bf16[2,32,128,128]{3,2,1,0:T(8,128)(2,1)S(1)} %cadzow.1, pred[2,32]{1,0:T(4,128)(4,1)S(1)} %add_compare_fusion), kind=kLoop, calls=%fused_computation | loop fusion | flops 6291456 | bytes 8388672 | tf_op jit(solution)/shard_map/jit(_where)/select_n | solution.py:514
  (1 shorter events, 0.0 us)
Async XLA Ops:
  1.6 1.6 %copy-start = (bf16[2,32,128,128]{3,2,1,0:T(8,128)(2,1)S(1)}, bf16[2,32,128,128]{3,2,1,0:T(8,128)(2,1)}, u32[]{:S(2)}) copy-start(bf16[2,32,128,128]{3,2,1,0:T(8,128)(2,1)} %param.2) | copy-start | bytes 6291460

commit v2 on v1

v2 whole, which is shorter than its diff:
```python
import functools

import jax
import jax.numpy as jnp
from jax import lax
from jax.experimental import pallas as pl
from jax.experimental.pallas import tpu as pltpu
from jax.sharding import PartitionSpec as P

NS_STEPS = 8
norm_floor = 1e-06
highest = lax.Precision.HIGHEST
MESH = pl.DeviceIdType.MESH
KH = 32
B = 128
f32, bf16 = jnp.float32, jnp.bfloat16
NT_DIMS = (((1,), (1,)), ((), ()))


def mm(left, right, **kw):
    return jnp.dot(left, right, preferred_element_type=f32, **kw)


def mm_nt(left, right, **kw):
    return lax.dot_general(left, right, NT_DIMS, preferred_element_type=f32, **kw)


def kernel(
    X, C, nb, SDT,
    l_ref, om_ref, out_ref,
    wl, q, omp, acc, s_send, s_recv, s_full, g_own, gx_recv, g_x, gc_recv, p_ref,
    bp, bpt, pacc, pr_send, pr_recv, prb, prx, tot, tx_send, tx_recv, ch, xr,
    l_sem, om_s, om_r, s_s, s_r, sx_s, sx_r, gx_s, gx_r, gc_s, gc_r, b_s, b_r,
    pr_s, pr_r, pa_s, pa_r, tx_s, tx_r, xr_s, xr_r, ag_s, ag_r, fx_s, fx_r,
):
    NT = nb // 2
    HB = NT // 2
    PO = nb // C
    PQ = NT // X
    LQ = NT // X
    r = lax.axis_index("row")
    c = lax.axis_index("col")
    x, core = r // 2, r % 2

    def dev(xx, cc, kk=None):
        return (xx * 2 + (core if kk is None else kk), cc)

    def col(dc):
        return lax.rem(c + dc + 4 * C, C)

    def xat(dx):
        return lax.rem(x + dx, X)

    def xcol(dx, delta):
        xx = xat(dx)
        return dev(xx, lax.rem(c + 2 * (xx - x) + delta + 4 * C, C))

    def remote(src, dst, send, recv, device):
        return pltpu.make_async_remote_copy(
            src_ref=src, dst_ref=dst, send_sem=send, recv_sem=recv, device_id=device, device_id_type=MESH
        )

    halves = [jnp.where(c - 2 * x - e < 0, 1, 0).astype(jnp.int32) for e in range(3)]

    barrier = pltpu.get_barrier_semaphore()
    peers = [dev(x, col(dc)) for dc in range(1, C)]
    for dx in range(1, X):
        peers += [xcol(dx, delta) for delta in (-1, 0, 1)] + [dev(xat(dx), c)]
    peers.append(dev(x, c, 1 - core))
    for peer in peers:
        pl.semaphore_signal(barrier, inc=1, device_id=peer, device_id_type=MESH)

    loads = []
    for h in range(2):
        for s in range(2):
            loads.append(
                pltpu.make_async_copy(
                    l_ref.at[h],
                    wl.at[h, pl.ds((1 + s) * B, nb * B), pl.ds(s * B, B)],
                    l_sem.at[2 * h + s],
                )
            )
    for cp in loads:
        cp.start()
    half_rank = pl.ds(pl.multiple_of(core * KH, KH), KH)
    for w in range(NT):
        n = NT - 1 - w
        q[n * KH : (n + 1) * KH, :B] = om_ref[half_rank, (2 * w + 1) * B : (2 * w + 2) * B]
        q[n * KH : (n + 1) * KH, B:] = om_ref[half_rank, 2 * w * B : (2 * w + 1) * B]
    zero = jnp.zeros((B, B), bf16)
    for h in range(2):
        wl[h, 0:B, 0:B] = zero
        wl[h, 0:B, B:] = zero
        wl[h, B : 2 * B, B:] = zero
        wl[h, (nb + 1) * B :, 0:B] = zero
    bp[0 : NT * KH, :] = jnp.zeros((NT * KH, 2 * B), bf16)
    bp[3 * NT * KH :, :] = jnp.zeros((NT * KH, 2 * B), bf16)
    PAD = PQ - 1
    for e in range(3):
        omp[e, 0 : PAD * KH, :] = jnp.zeros((PAD * KH, 2 * B), bf16)
        omp[e, (PAD + NT) * KH :, :] = jnp.zeros((PAD * KH, 2 * B), bf16)
    pl.semaphore_wait(barrier, len(peers))

    pending = []

    om_self = [lax.rem(2 * x + e, C) == 0 for e in range(3)]
    om_copies = []
    for e in range(3):
        cp = remote(q, omp.at[e, pl.ds(PAD * KH, NT * KH)], om_s.at[e], om_r.at[e], dev(x, col(2 * x + e)))
        om_copies.append(cp)

        @pl.when(jnp.logical_not(om_self[e]))
        def _():
            cp.start()

        @pl.when(om_self[e])
        def _():
            omp[e, PAD * KH : (PAD + NT) * KH, :] = q[...]

    for cp in loads:
        cp.wait()

    def lags(e, tau):
        return wl[halves[e], tau * 2 * B : (tau + 1) * 2 * B, :]

    srows, brows = PO * KH, PQ * KH
    s_copies = []

    def send_sketch(first, last):
        for dst in range(first, last):
            dc = lax.rem(dst - c + C, C)
            cp = remote(
                s_send.at[pl.ds(dst * srows, srows)], s_recv.at[dc], s_s.at[dc], s_r.at[dc], dev(x, dst)
            )
            pl.when(dst != c)(cp.start)

    started = set()
    for e in range(3):
        @pl.when(jnp.logical_not(om_self[e]))
        def _():
            om_copies[e].wait_recv()

        for b in range(0, 2 * NT, PQ):
            value = None
            for tau in range(NT + 1):
                n = b + NT - tau - e * NT
                if -PQ < n < NT:
                    left = omp[e, (PAD + n) * KH : (PAD + n) * KH + brows, :]
                    term = mm_nt(left, lags(e, tau))
                    value = term if value is None else value + term
            if value is None:
                continue
            rows = slice(b * KH, b * KH + brows)
            if b in started:
                value = value + acc[rows, :]
            started.add(b)
            acc[rows, :] = value
            if (e == 1 and b < NT) or e == 2:
                s_send[rows, :] = value.astype(SDT)
        if e > 0:
            send_sketch((e - 1) * C // 2, e * C // 2)

    for dc in range(1, C):
        s_copies.append(
            remote(s_send.at[pl.ds(0, srows)], s_recv.at[dc], s_s.at[dc], s_r.at[dc], dev(x, col(dc)))
        )
    total = acc[pl.ds(pl.multiple_of(c * srows, srows), srows), :]
    for dc in range(1, C):
        s_copies[dc - 1].wait_recv()
        total = total + s_recv[dc].astype(f32)
    pending += s_copies
    s_full[core] = total
    cp = remote(s_full.at[core], s_full.at[core], sx_s, sx_r, dev(x, c, 1 - core))
    cp.start()
    cp.wait_recv()
    pending.append(cp)

    sk = jnp.concatenate(
        [
            jnp.concatenate([s_full[k, o * KH : (o + 1) * KH, :] for k in range(2)], axis=0)
            for o in range(PO)
        ],
        axis=1,
    )
    gram = mm_nt(sk, sk, precision=highest)
    g_own[...] = jnp.concatenate([gram[:KH], gram[KH:]], axis=1)
    copies = []
    for dx in range(1, X):
        cp = remote(g_own, gx_recv.at[dx], gx_s.at[dx], gx_r.at[dx], dev(xat(dx), c))
        cp.start()
        copies.append(cp)
    packed = g_own[...]
    for dx in range(1, X):
        copies[dx - 1].wait_recv()
        packed = packed + gx_recv[dx]
    pending += copies
    g_x[...] = packed
    copies = []
    for dc in range(1, C):
        cp = remote(g_x, gc_recv.at[dc], gc_s.at[dc], gc_r.at[dc], dev(x, col(dc)))
        cp.start()
        copies.append(cp)
    for dc in range(1, C):
        copies[dc - 1].wait_recv()
        packed = packed + gc_recv[dc]
    pending += copies
    gram = jnp.concatenate([packed[:, : 2 * KH], packed[:, 2 * KH :]], axis=0)

    eye = (
        lax.broadcasted_iota(jnp.int32, (2 * KH, 2 * KH), 0)
        == lax.broadcasted_iota(jnp.int32, (2 * KH, 2 * KH), 1)
    ).astype(f32)
    trace = jnp.sum(gram * eye)
    scale = 1.0 / jnp.sqrt(jnp.full((1, 1), trace, f32) + norm_floor)
    inner = gram * (scale * scale)
    prod = None
    for sweep in range(NS_STEPS):
        a = 1.5 * eye - 0.5 * inner
        prod = a if prod is None else mm(prod, a, precision=highest)
        if sweep < NS_STEPS - 1:
            inner = mm(a, mm(inner, a, precision=highest), precision=highest)
    p_ref[...] = prod * scale

    basis = mm(p_ref[pl.ds(pl.multiple_of(core * KH, KH), KH), :], sk, precision=highest).astype(bf16)
    mine = pl.multiple_of((NT + c * PO) * KH, KH)
    for o in range(PO):
        bp[pl.ds(pl.multiple_of(mine + o * KH, KH), KH), :] = basis[:, o * 2 * B : (o + 1) * 2 * B]
    copies = []
    for dc in range(1, C):
        at = bp.at[pl.ds(mine, srows)]
        cp = remote(at, at, b_s.at[dc], b_r.at[dc], dev(x, col(dc)))
        cp.start()
        copies.append(cp)
    for cp in copies:
        cp.wait_recv()
    pending += copies

    qrows = PQ * KH
    pr_copies = {}
    for dx in range(X):
        for e in range(3):
            if dx > 0 or e != 1:
                slot = dx * 3 + e
                pr_copies[slot] = remote(
                    pr_send.at[e, pl.ds(0, qrows)], pr_recv.at[slot], pr_s.at[slot], pr_r.at[slot],
                    xcol(dx, 1 - e),
                )
    for e in (0, 2, 1):
        for b in range(0, NT, PQ):
            value = None
            for tau in range(NT + 1):
                if (e == 0 and b + PQ - 1 < NT - tau) or (e == 2 and b >= NT - tau):
                    continue
                first = (e * NT + b + tau) * KH
                term = mm(bp[first : first + qrows, :], lags(e, tau))
                value = term if value is None else value + term
            rows = slice(b * KH, b * KH + qrows)
            pr_send[e, rows, :] = value.astype(bf16)
            if e == 1:
                pacc[rows, :] = value
            owner = b // PQ
            dx = lax.rem(owner - x + X, X)
            slot = dx * 3 + e
            cp = remote(
                pr_send.at[e, pl.ds(b * KH, qrows)], pr_recv.at[slot], pr_s.at[slot], pr_r.at[slot],
                dev(owner, lax.rem(c + 2 * (owner - x) + 1 - e + 4 * C, C)),
            )
            if e == 1:
                pl.when(owner != x)(cp.start)
            else:
                cp.start()

    for g in range(NT):
        first = (NT + 2 * g) * KH
        pieces = [
            bp[first + o * KH : first + (o + 1) * KH, s * B : (s + 1) * B] for o in range(2) for s in range(2)
        ]
        bpt[:, g * B : (g + 1) * B] = jnp.concatenate(pieces, axis=0).T

    quarter = pl.ds(pl.multiple_of(x * qrows, qrows), qrows)
    total = pacc[quarter, :]
    for slot, cp in pr_copies.items():
        cp.wait_recv()
        total = total + pr_recv[slot].astype(f32)
    pending += list(pr_copies.values())
    prb[1, quarter, :] = total.astype(bf16)
    copies = []
    for dx in range(X):
        for e in range(3):
            if dx == 0 and e == 1:
                continue
            slot = dx * 3 + e
            cp = remote(
                prb.at[1, quarter], prb.at[e, quarter], pa_s.at[slot], pa_r.at[slot], xcol(dx, e - 1)
            )
            cp.start()
            copies.append(cp)
    for cp in copies:
        cp.wait_recv()
    pending += copies

    def active(h, xx):
        return c - 2 * xx >= 0 if h == 0 else c - 2 * xx - 2 < 0

    nbr, nbc = 2 * nb * X, nb * C

    def lag_of(h, t):
        return h * nbc + c * nb + core * NT + t

    def pairs_of(lag, first, last):
        low = jnp.maximum(first, lag - (nbc - 1))
        return jnp.maximum(jnp.minimum(last, lag) - low + 1, 0).astype(f32)

    def measured(h, t):
        return wl[h, pl.ds(pl.multiple_of((core * NT + t + 1) * B, B), B), 0:B].astype(f32)

    order = sorted(range(1, X), key=lambda dx: -min(dx, X - dx)) + [0]
    tx_copies, xr_sends = [], []
    for h in range(2):
        across, sends = [], {}
        for k, dx in enumerate(order):
            across.append(
                remote(
                    tx_send.at[h, k], tx_recv.at[h, k], tx_s.at[h * X + k], tx_r.at[h * X + k],
                    dev(x, c, 1 - core),
                )
            )
            if dx > 0:
                sends[dx] = remote(
                    ch.at[h, k], xr.at[h, dx], xr_s.at[h * X + dx], xr_r.at[h * X + dx], dev(xat(dx), c)
                )
        tx_copies.append(across)
        xr_sends.append(sends)

        @pl.when(active(h, x))
        def _():
            for e in range(3):
                @pl.when(halves[e] == h)
                def _():
                    for i in range(NT):
                        n = e * NT + i
                        pair = prb[e, i * KH : (i + 1) * KH, :]
                        prx[n, 0:KH, :] = pair
                        prx[n, KH:, :B] = pair[:, B:]
                        if n > 0:
                            prx[n - 1, KH:, B:] = pair[:, :B]

                @pl.when(halves[e] != h)
                def _():
                    for i in range(NT):
                        n = e * NT + i
                        prx[n, 0:KH, :] = jnp.zeros((KH, 2 * B), bf16)
                        prx[n, KH:, :B] = jnp.zeros((KH, B), bf16)
                        if n > 0:
                            prx[n - 1, KH:, B:] = jnp.zeros((KH, B), bf16)

            def lag_pair(tp):
                right = prx[pl.ds(NT - 1 - tp, 2 * NT)].reshape(4 * NT * KH, 2 * B)
                return mm(bpt[...], right)

            def combine(k):
                dx = order[k]
                across[k].wait_recv()
                for i in range(LQ):
                    t = xat(dx) * LQ + i
                    n = pairs_of(lag_of(h, t), 2 * nb * x, 2 * nb * (x + 1) - 1)
                    value = tot[h, k, i] + tx_recv[h, k, i].astype(f32) - (0.5 * n) * measured(h, t)
                    if dx > 0:
                        ch[h, k, i] = value.astype(bf16)
                    else:
                        tot[h, k, i] = value
                if dx > 0:
                    sends[dx].start()

            for k, dx in enumerate(order):
                first = xat(dx) * (LQ // 2)
                for i in range(LQ // 2):
                    value = lag_pair((1 - core) * HB + first + i).astype(bf16)
                    tx_send[h, k, 2 * i] = value[:, B:]
                    tx_send[h, k, 2 * i + 1] = value[:, :B]
                across[k].start()
                for i in range(LQ // 2):
                    value = lag_pair(core * HB + first + i)
                    tot[h, k, 2 * i] = value[:, B:]
                    tot[h, k, 2 * i + 1] = value[:, :B]
                if k > 0:
                    combine(k - 1)
            combine(X - 1)

    has = [None, c < 2 * X]
    ag_copies, fx_copies = [], []

    def piece(h, xx):
        return out_ref.at[h, pl.ds(core * NT + xx * LQ, LQ)]

    for h in range(2):
        ag_copies.append(
            [
                remote(piece(h, x), piece(h, x), ag_s.at[h * X + dx], ag_r.at[h * X + dx], dev(xat(dx), c))
                for dx in range(1, X)
            ]
        )
        fx_copies.append(
            [
                remote(
                    piece(h, lax.rem(x - dx + X, X)), piece(h, lax.rem(x - dx + X, X)),
                    fx_s.at[h * X + dx], fx_r.at[h * X + dx], dev(x, c, 1 - core),
                )
                for dx in range(X)
            ]
        )

    def spread(h):
        @pl.when(jnp.logical_not(active(h, x)))
        def _():
            tot[h, X - 1] = jnp.zeros((LQ, B, B), f32)

        for dx in range(1, X):
            @pl.when(active(h, lax.rem(x - dx + X, X)))
            def _():
                xr_sends[h][dx].wait_recv()
                tot[h, X - 1] += xr[h, dx].astype(f32)

        for i in range(LQ):
            t = x * LQ + i
            n = pairs_of(lag_of(h, t), 0, nbr - 1)
            out_ref[h, core * NT + t] = (tot[h, X - 1, i] * (1.0 / jnp.maximum(n, 1.0))).astype(bf16)
        for cp in ag_copies[h]:
            cp.start()
        fx_copies[h][0].start()

    def gather(h):
        for dx in range(1, X):
            ag_copies[h][dx - 1].wait_recv()
            fx_copies[h][dx].start()

    def settle(h):
        for cp in fx_copies[h]:
            cp.wait_recv()
        for cp in ag_copies[h] + fx_copies[h]:
            cp.wait_send()

    for part in (spread, gather, settle):
        part(0)
        pl.when(has[1])(functools.partial(part, 1))

    @pl.when(jnp.logical_not(has[1]))
    def _():
        out_ref[1] = jnp.zeros((nb, B, B), bf16)

    for h in range(2):
        @pl.when(active(h, x))
        def _():
            for cp in tx_copies[h] + list(xr_sends[h].values()):
                cp.wait_send()

    for e in range(3):
        @pl.when(jnp.logical_not(om_self[e]))
        def _():
            om_copies[e].wait_send()

    for cp in pending:
        cp.wait_send()


def local(X, C, SDT, markov, omega):
    halves, nb = markov.shape[:2]
    NT = nb // 2
    PO, PQ, LQ = nb // C, NT // X, NT // X
    vmem, dma = pltpu.VMEM, pltpu.SemaphoreType.DMA
    scratch = [
        vmem((2, (nb + 2) * B, 2 * B), bf16),
        vmem((NT * KH, 2 * B), bf16),
        vmem((3, (NT + 2 * PQ - 2) * KH, 2 * B), bf16),
        vmem((2 * NT * KH, 2 * B), f32),
        vmem((2 * NT * KH, 2 * B), SDT),
        vmem((C, PO * KH, 2 * B), SDT),
        vmem((2, PO * KH, 2 * B), f32),
        vmem((KH, 4 * KH), f32),
        vmem((X, KH, 4 * KH), f32),
        vmem((KH, 4 * KH), f32),
        vmem((C, KH, 4 * KH), f32),
        vmem((2 * KH, 2 * KH), f32),
        vmem((4 * NT * KH, 2 * B), bf16),
        vmem((B, NT * B), bf16),
        vmem((NT * KH, 2 * B), f32),
        vmem((3, NT * KH, 2 * B), bf16),
        vmem((3 * X, PQ * KH, 2 * B), bf16),
        vmem((3, NT * KH, 2 * B), bf16),
        vmem((3 * NT, 2 * KH, 2 * B), bf16),
        vmem((2, X, LQ, B, B), f32),
        vmem((2, X, LQ, B, B), bf16),
        vmem((2, X, LQ, B, B), bf16),
        vmem((2, X, LQ, B, B), bf16),
        vmem((2, X, LQ, B, B), bf16),
        dma((4,)),
        dma((3,)), dma((3,)), dma((C,)), dma((C,)), dma, dma,
        dma((X,)), dma((X,)), dma((C,)), dma((C,)), dma((C,)), dma((C,)),
        dma((3 * X,)), dma((3 * X,)), dma((3 * X,)), dma((3 * X,)),
        *[dma((2 * X,))] * 8,
    ]
    excess = pl.pallas_call(
        functools.partial(kernel, X, C, nb, SDT),
        out_shape=jax.ShapeDtypeStruct((halves, nb, B, B), bf16),
        in_specs=[pl.BlockSpec(memory_space=pl.ANY), pl.BlockSpec(memory_space=pltpu.VMEM)],
        out_specs=pl.BlockSpec(memory_space=pltpu.VMEM),
        scratch_shapes=scratch,
        compiler_params=pltpu.CompilerParams(
            collective_id=0, has_side_effects=True, vmem_limit_bytes=48 * 2**20
        ),
        name="cadzow",
    )(markov.reshape(halves, nb * B, B), omega.T)
    lags = (
        jnp.arange(2, dtype=jnp.int32)[:, None] * (nb * C)
        + lax.axis_index("col") * nb
        + jnp.arange(nb, dtype=jnp.int32)[None, :]
    )
    counts = jnp.minimum(lags, 2 * nb * X - 1) - jnp.maximum(0, lags - nb * C + 1) + 1
    measured = markov.astype(f32)
    merged = 0.75 * measured + 0.5 * excess.astype(f32)
    return jnp.where((counts > 0)[:, :, None, None], merged, measured)


def solution(mesh):
    X, C = mesh.shape["row"] // 2, mesh.shape["col"]
    in_specs = (P(None, "col", None, None), P("col", None))
    return jax.shard_map(
        functools.partial(local, X, C, bf16),
        mesh=mesh,
        in_specs=in_specs,
        out_specs=P(None, "col", None, None),
        check_vma=False,
    )
```

time: 149 us -> 133 us (0.89)
  the two profiles are of different devices: /device:TPU:33 before, /device:TPU:25 now
where the time goes in v2:
time: 133 us
  Pallas kernels  127 us (95%)
  other arithmetic  3.24 us (2%)
  local copies, waits for them, and re-layouts  2.63 us (2%)
    pallas_call x1, Pallas kernels, local(): pl.pallas_call(functools.partial(kernel, X, C, nb, SDT), out_shape=jax.Sh...  127 us
    select_n x1, other arithmetic, local(): return jnp.where((counts > 0)[:, :, None, None], merged, measured)  3.15 us

profile of v2, /device:TPU:25, one launch (start us, length us, event | category | flops | bytes accessed | tf_op | source)
XLA Modules:
  0.0 132.9 jit_solution(6722179310939283166)
XLA Ops:
  0.0 0.1 add_compare_fusion
  0.1 0.0 copy-start
  0.1 1.6 %copy-done = bf16[2,32,128,128]{3,2,1,0:T(8,128)(2,1)S(1)} copy-done((bf16[2,32,128,128]{3,2,1,0:T(8,128)(2,1)S(1)}, bf16[2,32,128,128]{3,2,1,0:T(8,128)(2,1)}, u32[]{:S(2)}) %copy-start) | copy-done | bytes 2097176
  1.7 0.0 copy-start.1
  1.7 1.0 copy-done.1
  2.7 127.1 %cadzow.1 = bf16[2,32,128,128]{3,2,1,0:T(8,128)(2,1)S(1)} custom-call(bf16[2,4096,128]{2,1,0:T(8,128)(2,1)S(1)} %bitcast.2, bf16[64,4096]{1,0:T(8,128)(2,1)S(1)} %bitcast.3), custom_call_target="tpu_custom_call" | custom-call | tf_op jit(solution)/shard_map/cadzow/pallas_call | solution.py:502
  129.8 3.2 %convert_select_fusion = f32[2,32,128,128]{3,2,1,0:T(8,128)} fusion(bf16[2,32,128,128]{3,2,1,0:T(8,128)(2,1)S(1)} %copy-done, bf16[2,32,128,128]{3,2,1,0:T(8,128)(2,1)S(1)} %cadzow.1, pred[2,32]{1,0:T(4,128)(4,1)S(1)} %add_compare_fusion), kind=kLoop, calls=%fused_computation | loop fusion | flops 6291456 | bytes 8388672 | tf_op jit(solution)/shard_map/jit(_where)/select_n | solution.py:521
  (1 shorter events, 0.0 us)
Async XLA Ops:
  0.1 1.6 %copy-start = (bf16[2,32,128,128]{3,2,1,0:T(8,128)(2,1)S(1)}, bf16[2,32,128,128]{3,2,1,0:T(8,128)(2,1)}, u32[]{:S(2)}) copy-start(bf16[2,32,128,128]{3,2,1,0:T(8,128)(2,1)} %param.2) | copy-start | bytes 6291460
  1.7 1.0 copy-start.1

commit v3 on v2

--- a/solution.py
+++ b/solution.py
@@ -30,7 +30,7 @@
     l_ref, om_ref, out_ref,
     wl, q, omp, acc, s_send, s_recv, s_full, g_own, gx_recv, g_x, gc_recv, p_ref,
     bp, bpt, pacc, pr_send, pr_recv, prb, prx, tot, tx_send, tx_recv, ch, xr,
-    l_sem, om_s, om_r, s_s, s_r, sx_s, sx_r, gx_s, gx_r, gc_s, gc_r, b_s, b_r,
+    sg, l_sem, om_s, om_r, s_s, s_r, sx_s, sx_r, sw_s, sw_r, gx_s, gx_r, gc_s, gc_r, b_s, b_r,
     pr_s, pr_r, pa_s, pa_r, tx_s, tx_r, xr_s, xr_r, ag_s, ag_r, fx_s, fx_r,
 ):
     NT = nb // 2
@@ -170,10 +170,16 @@
         total = total + s_recv[dc].astype(f32)
     pending += s_copies
     s_full[core] = total
-    cp = remote(s_full.at[core], s_full.at[core], sx_s, sx_r, dev(x, c, 1 - core))
-    cp.start()
-    cp.wait_recv()
-    pending.append(cp)
+    over = remote(s_full.at[core], s_full.at[core], sx_s, sx_r, dev(x, c, 1 - core))
+    over.start()
+    mine = pl.ds(pl.multiple_of(c * srows, srows), srows)
+    sg[core, mine, :] = total.astype(bf16)
+    b_copies = []
+    for dc in range(1, C):
+        cp = remote(sg.at[core, mine], sg.at[core, mine], b_s.at[dc], b_r.at[dc], dev(x, col(dc)))
+        cp.start()
+        b_copies.append(cp)
+    over.wait_recv()
 
     sk = jnp.concatenate(
         [
@@ -184,26 +190,29 @@
     )
     gram = mm_nt(sk, sk, precision=highest)
     g_own[...] = jnp.concatenate([gram[:KH], gram[KH:]], axis=1)
-    copies = []
+    gx_copies = []
     for dx in range(1, X):
         cp = remote(g_own, gx_recv.at[dx], gx_s.at[dx], gx_r.at[dx], dev(xat(dx), c))
         cp.start()
-        copies.append(cp)
+        gx_copies.append(cp)
     packed = g_own[...]
     for dx in range(1, X):
-        copies[dx - 1].wait_recv()
+        gx_copies[dx - 1].wait_recv()
         packed = packed + gx_recv[dx]
-    pending += copies
     g_x[...] = packed
-    copies = []
+    gc_copies = []
     for dc in range(1, C):
         cp = remote(g_x, gc_recv.at[dc], gc_s.at[dc], gc_r.at[dc], dev(x, col(dc)))
         cp.start()
-        copies.append(cp)
+        gc_copies.append(cp)
+    for cp in b_copies:
+        cp.wait_recv()
+    whole = remote(sg.at[core], sg.at[core], sw_s, sw_r, dev(x, c, 1 - core))
+    whole.start()
     for dc in range(1, C):
-        copies[dc - 1].wait_recv()
+        gc_copies[dc - 1].wait_recv()
         packed = packed + gc_recv[dc]
-    pending += copies
+    pending += [over, *gx_copies, *b_copies, *gc_copies, whole]
     gram = jnp.concatenate([packed[:, : 2 * KH], packed[:, 2 * KH :]], axis=0)
 
     eye = (
@@ -220,20 +229,18 @@
         if sweep < NS_STEPS - 1:
             inner = mm(a, mm(inner, a, precision=highest), precision=highest)
     p_ref[...] = prod * scale
-
-    basis = mm(p_ref[pl.ds(pl.multiple_of(core * KH, KH), KH), :], sk, precision=highest).astype(bf16)
-    mine = pl.multiple_of((NT + c * PO) * KH, KH)
-    for o in range(PO):
-        bp[pl.ds(pl.multiple_of(mine + o * KH, KH), KH), :] = basis[:, o * 2 * B : (o + 1) * 2 * B]
-    copies = []
-    for dc in range(1, C):
-        at = bp.at[pl.ds(mine, srows)]
-        cp = remote(at, at, b_s.at[dc], b_r.at[dc], dev(x, col(dc)))
-        cp.start()
-        copies.append(cp)
-    for cp in copies:
-        cp.wait_recv()
-    pending += copies
+    weights = p_ref[half_rank, :]
+    w1 = weights.astype(bf16)
+    rest = weights - w1.astype(f32)
+    w2 = rest.astype(bf16)
+    w3 = (rest - w2.astype(f32)).astype(bf16)
+    whole.wait_recv()
+    stack = jnp.concatenate([w1, w2, w3], axis=0)
+    for n in range(2 * NT):
+        both = jnp.concatenate([sg[k, n * KH : (n + 1) * KH, :] for k in range(2)], axis=0)
+        three = mm(stack, both)
+        value = three[:KH] + three[KH : 2 * KH] + three[2 * KH :]
+        bp[(NT + n) * KH : (NT + n + 1) * KH, :] = value.astype(bf16)
 
     qrows = PQ * KH
     pr_copies = {}
@@ -493,8 +500,9 @@
         vmem((2, X, LQ, B, B), bf16),
         vmem((2, X, LQ, B, B), bf16),
         vmem((2, X, LQ, B, B), bf16),
+        vmem((2, 2 * NT * KH, 2 * B), bf16),
         dma((4,)),
-        dma((3,)), dma((3,)), dma((C,)), dma((C,)), dma, dma,
+        dma((3,)), dma((3,)), dma((C,)), dma((C,)), dma, dma, dma, dma,
         dma((X,)), dma((X,)), dma((C,)), dma((C,)), dma((C,)), dma((C,)),
         dma((3 * X,)), dma((3 * X,)), dma((3 * X,)), dma((3 * X,)),
         *[dma((2 * X,))] * 8,

time: 133 us -> 130 us (0.977)
  Pallas kernels: 127 us -> 124 us
    pallas_call x1, Pallas kernels: 127 us -> 124 us  [local(): pl.pallas_call(functools.partial(kernel, X, C, nb, SDT), out_shape=jax.Sh...]
where the time goes in v3:
time: 130 us
  Pallas kernels  124 us (95%)
  other arithmetic  3.24 us (2%)
  local copies, waits for them, and re-layouts  2.63 us (2%)
    pallas_call x1, Pallas kernels, local(): pl.pallas_call(functools.partial(kernel, X, C, nb, SDT), out_shape=jax.Sh...  124 us
    select_n x1, other arithmetic, local(): return jnp.where((counts > 0)[:, :, None, None], merged, measured)  3.15 us
    unnamed x4, local copies, waits for them, and re-layouts  2.63 us

profile of v3, /device:TPU:25, one launch (start us, length us, event | category | flops | bytes accessed | tf_op | source)
XLA Modules:
  0.0 129.9 jit_solution(1124762773520824685)
XLA Ops:
  0.0 0.1 add_compare_fusion
  0.1 0.0 copy-start
  0.1 1.6 %copy-done = bf16[2,32,128,128]{3,2,1,0:T(8,128)(2,1)S(1)} copy-done((bf16[2,32,128,128]{3,2,1,0:T(8,128)(2,1)S(1)}, bf16[2,32,128,128]{3,2,1,0:T(8,128)(2,1)}, u32[]{:S(2)}) %copy-start) | copy-done | bytes 2097176
  1.7 0.0 copy-start.1
  1.7 1.0 copy-done.1
  2.7 124.0 %cadzow.1 = bf16[2,32,128,128]{3,2,1,0:T(8,128)(2,1)S(1)} custom-call(bf16[2,4096,128]{2,1,0:T(8,128)(2,1)S(1)} %bitcast.2, bf16[64,4096]{1,0:T(8,128)(2,1)S(1)} %bitcast.3), custom_call_target="tpu_custom_call" | custom-call | tf_op jit(solution)/shard_map/cadzow/pallas_call | solution.py:510
  126.8 3.2 %convert_select_fusion = f32[2,32,128,128]{3,2,1,0:T(8,128)} fusion(bf16[2,32,128,128]{3,2,1,0:T(8,128)(2,1)S(1)} %copy-done, bf16[2,32,128,128]{3,2,1,0:T(8,128)(2,1)S(1)} %cadzow.1, pred[2,32]{1,0:T(4,128)(4,1)S(1)} %add_compare_fusion), kind=kLoop, calls=%fused_computation | loop fusion | flops 6291456 | bytes 8388672 | tf_op jit(solution)/shard_map/jit(_where)/select_n | solution.py:529
  (1 shorter events, 0.0 us)
Async XLA Ops:
  0.1 1.6 %copy-start = (bf16[2,32,128,128]{3,2,1,0:T(8,128)(2,1)S(1)}, bf16[2,32,128,128]{3,2,1,0:T(8,128)(2,1)}, u32[]{:S(2)}) copy-start(bf16[2,32,128,128]{3,2,1,0:T(8,128)(2,1)} %param.2) | copy-start | bytes 6291460
  1.7 1.0 copy-start.1
